TPU v7x, 512 devices: a whole 4x4x16 slice. The times are simulated.
512 devices in a mesh: group: 16 (over x_lo, y, core), tensor: 32 (over z, x_hi).
Axes of the slice: x: 4 (x_hi: 2, x_lo: 2; x = x_hi * 2 + x_lo), y: 4, z: 16, core: 2. Of those that a mesh axis runs over, the one named last changes fastest.
Arguments:
- hidden_in: bfloat16 [4, 4096, 5120], P(None, 'group', 'tensor'), may hold values from -6 to 6
- norm_gain: float32 [5120], replicated, may hold values from 0.25 to 1.75
- q_weight: bfloat16 [5120, 4096], P(None, 'tensor'), may hold values from -0.078125 to 0.078125
- q_gain: float32 [128], replicated, may hold values from 0.25 to 1.75
- o_weight: bfloat16 [4096, 5120], P(None, 'tensor'), may hold values from -0.09375 to 0.09375
- kv_cache: bfloat16 [2, 4096, 8, 512], P(None, 'group'), may hold values from -600 to 600
- positions: int32 [4, 4096], P(None, 'group'), may hold values from 0 to 4095
- grad_down: bfloat16 [16, 64, 5120], P('group', None, 'tensor'), may hold values from -6 to 6
- grad_up: bfloat16 [16, 64, 4096], P('group', None, 'tensor'), may hold values from -6 to 6
- down_param: float32 [64, 5120], P(None, 'tensor'), may hold values from -5 to 5
- down_first: float32 [64, 5120], P(None, 'tensor'), may hold values from -4 to 4
- down_second: float32 [64, 5120], P(None, 'tensor'), may hold values from 0.01 to 0.5
- up_param: float32 [64, 4096], P(None, 'tensor'), may hold values from -5 to 5
- up_first: float32 [64, 4096], P(None, 'tensor'), may hold values from -4 to 4
- up_second: float32 [64, 4096], P(None, 'tensor'), may hold values from 0.01 to 0.5
Outputs:
- new_down: float32 [64, 5120], P(None, 'tensor')
- new_up: float32 [64, 4096], P(None, 'tensor')
- decoded: bfloat16 [4, 4096, 5120], P(None, 'group', 'tensor')
All inputs are finite; a program needn't handle non-finite values.
Results may differ from a plain program's by a relative error of at most 0.012.
The roundings to bfloat16 on the way count: a program that leaves them out, or rounds other values in their place, can miss the bound.
Values may be sent and summed in bfloat16 or wider, within the bound.
A program may use at most 64 MiB of HBM per device.

v0:
```python
import jax
import jax.numpy as jnp
from jax import lax
from jax.sharding import PartitionSpec as P

beta_first = 0.9
beta_second = 0.999
first_fix = 0.9999734386
second_fix = 0.095207851
learn_rate = 0.5
decay_rate = 0.01
adam_eps = 1e-08
norm_eps = 1e-06
rope_base = 1000000.0


def adamw(param, first, second, grad):
    first_new = beta_first * first + (1.0 - beta_first) * grad
    second_new = beta_second * second + (1.0 - beta_second) * grad * grad
    first_hat = first_new / first_fix
    second_hat = second_new / second_fix
    return param - learn_rate * (first_hat / (jnp.sqrt(second_hat) + adam_eps) + decay_rate * param)


def rotary(query, angle):
    half = query.shape[-1] // 2
    cosine = jnp.cos(angle)
    sine = jnp.sin(angle)
    cosine = jnp.concatenate([cosine, cosine], axis=-1)
    sine = jnp.concatenate([sine, sine], axis=-1)
    turned = jnp.concatenate([-query[..., half:], query[..., :half]], axis=-1)
    return query * cosine + turned * sine


def body(
    hidden_in,
    norm_gain,
    q_weight,
    q_gain,
    o_weight,
    kv_cache,
    positions,
    grad_down,
    grad_up,
    down_param,
    down_first,
    down_second,
    up_param,
    up_first,
    up_second,
):
    steps_here, rows_here, local_width = hidden_in.shape
    width = q_weight.shape[0]
    head_size = q_weight.shape[1]
    rank = down_param.shape[0]
    down_part = grad_down[0].astype(jnp.float32)
    up_part = grad_up[0].astype(jnp.float32)
    down_total, up_total = lax.psum((down_part, up_part), "group")
    new_down = adamw(down_param, down_first, down_second, down_total)
    new_up = adamw(up_param, up_first, up_second, up_total)
    scale = 1.0 / jnp.sqrt(jnp.float32(rank * width))
    base_rows = q_weight.astype(jnp.float32)
    delta = jnp.einsum(
        "rd,rc->dc",
        lax.all_gather(new_down, "tensor", axis=1, tiled=True),
        new_up,
        precision=lax.Precision.HIGHEST,
        preferred_element_type=jnp.float32,
    )
    merged = (base_rows + scale * delta).astype(jnp.bfloat16)
    stream_local = hidden_in.astype(jnp.float32)
    stream_full = lax.all_gather(hidden_in, "tensor", axis=2, tiled=True).astype(jnp.float32)
    inverse = lax.rsqrt(jnp.mean(stream_full * stream_full, axis=-1, keepdims=True) + norm_eps)
    normed = (stream_full * inverse * norm_gain).astype(jnp.bfloat16)
    query = jnp.dot(
        normed.reshape(steps_here * rows_here, width), merged, preferred_element_type=jnp.float32
    )
    query = query.reshape(steps_here, rows_here, head_size)
    qinv = lax.rsqrt(jnp.mean(query * query, axis=-1, keepdims=True) + norm_eps)
    query = query * qinv * q_gain
    freq = rope_base ** (-2.0 * jnp.arange(head_size // 2, dtype=jnp.float32) / head_size)
    angle = positions.astype(jnp.float32)[:, :, None] * freq
    rotated = rotary(query, angle).astype(jnp.bfloat16)
    kv_start = lax.axis_index("tensor") // 8 * head_size
    kv_local = lax.dynamic_slice_in_dim(kv_cache, kv_start, head_size, 3)
    scores = jnp.einsum(
        "srd,rcd->src", rotated, kv_local[0], preferred_element_type=jnp.float32
    ) / jnp.sqrt(jnp.float32(head_size))
    top = jnp.max(scores, axis=-1, keepdims=True)
    expo = jnp.exp(scores - top)
    weights = (expo / jnp.sum(expo, axis=-1, keepdims=True)).astype(jnp.bfloat16)
    heads_out = jnp.einsum(
        "src,rcd->srd", weights, kv_local[1], preferred_element_type=jnp.float32
    ).astype(jnp.bfloat16)
    heads_out = heads_out.reshape(steps_here * rows_here, head_size)
    projected = jnp.dot(
        lax.all_gather(heads_out, "tensor", axis=1, tiled=True),
        o_weight,
        preferred_element_type=jnp.float32,
    )
    decoded = (stream_local + projected.reshape(steps_here, rows_here, local_width)).astype(
        jnp.bfloat16
    )
    return (new_down, new_up, decoded)


def solution(mesh):
    in_specs = (
        P(None, "group", "tensor"),
        P(),
        P(None, "tensor"),
        P(),
        P(None, "tensor"),
        P(None, "group", None, None),
        P(None, "group"),
        P("group", None, "tensor"),
        P("group", None, "tensor"),
        P(None, "tensor"),
        P(None, "tensor"),
        P(None, "tensor"),
        P(None, "tensor"),
        P(None, "tensor"),
        P(None, "tensor"),
    )
    out_specs = (P(None, "tensor"), P(None, "tensor"), P(None, "group", "tensor"))
    return jax.shard_map(body, mesh=mesh, in_specs=in_specs, out_specs=out_specs, check_vma=False)
```

profile of v0, /device:TPU:1, one launch (start us, length us, event | category | flops | bytes accessed | tf_op | source)
XLA Modules:
  0.0 729.6 jit_solution(2244260567174859330)
XLA Ops:
  7.2 1.5 bitcast_convert_fusion
  8.7 1.3 bitcast_convert_fusion.1
  10.1 133.2 %all-reduce.3.cloned.1.call-done = (f32[64,160]{1,0:T(8,128)}, f32[64,128]{1,0:T(8,128)}) async-done(((f32[64,160]{1,0:T(8,128)}, f32[64,128]{1,0:T(8,128)}), (f32[64,160]{1,0:T(8,128)}, f32[64,128]{1,0:T(8,128)})) %all-reduce.3.cloned.1.call-update) | async-done | bytes 73744 | tf_op jit(solution)/shard_map/psum | solution.py:58
  143.3 1.6 multiply_subtract_fusion
  145.0 0.7 all-gather.5.cloned.1.call-update
  145.7 0.7 convert_element_type.54
  146.4 1.8 multiply_sine_fusion
  148.2 0.8 multiply_subtract_fusion.1
  149.1 140.6 %all-gather.9.cloned.1.call-done = f32[32,160,64]{1,2,0:T(8,128)} async-done(((f32[1,160,64]{1,2,0:T(8,128)}), f32[32,160,64]{1,2,0:T(8,128)}) %all-gather.9.cloned.1.call-update) | async-done | bytes 1310736 | tf_op jit(solution)/shard_map/all_gather | solution.py:65
  289.7 2.8 copy.28
  292.5 2.7 reshape.51
  295.3 6.0 fusion.10
  301.3 197.6 %all-gather.5.cloned.1.call-done = bf16[4,256,5120]{1,2,0:T(8,128)(2,1)} async-done(((bf16[4,256,160]{1,2,0:T(8,128)(2,1)}), bf16[4,256,5120]{1,2,0:T(8,128)(2,1)}) %all-gather.5.cloned.1.call-update) | async-done | bytes 10485776 | tf_op jit(solution)/shard_map/all_gather | solution.py:72
  498.8 6.2 fusion.1
  505.0 0.8 copy-done.1
  505.8 3.4 multiply_reduce_fusion
  509.4 0.2 fusion.17
  509.6 0.2 copy.31
  509.8 1.8 fusion.37
  511.6 1.6 fusion.14
  513.2 0.7 copy.32
  514.0 202.0 %all-gather.7.cloned.1.call-done = bf16[1024,4096]{1,0:T(8,128)(2,1)} async-done(((bf16[1024,128]{1,0:T(8,128)(2,1)}), bf16[1024,4096]{1,0:T(8,128)(2,1)}) %all-gather.7.cloned.1.call-update) | async-done | bytes 8388624 | tf_op jit(solution)/shard_map/all_gather | solution.py:97
  715.9 6.3 fusion.38
  722.2 0.8 fusion.15
  (27 shorter events, 0.4 us)
Async XLA Ops:
  7.2 708.8 %copy-start = (bf16[4096,160]{0,1:T(8,128)(2,1)S(1)}, bf16[4096,160]{0,1:T(8,128)(2,1)}, u32[]{:S(2)}) copy-start(bf16[4096,160]{0,1:T(8,128)(2,1)} %param.19) | copy-start | bytes 3932164
  7.2 136.1 %all-reduce.3.cloned.1.call-start = ((), (), s32[]{:S(2)}) async-start(), calls=%async_computation.3 | async-start | bytes 196608 | tf_op jit(solution)/shard_map/psum | solution.py:58
  10.1 279.7 %all-gather.9.cloned.1.call-start = ((), (), s32[]{:S(2)}) async-start(), calls=%async_computation.2 | async-start | bytes 2162688 | tf_op jit(solution)/shard_map/all_gather | solution.py:65
  144.9 353.9 %all-gather.5.cloned.1.call-start = ((), (), s32[]{:S(2)}) async-start(), calls=%async_computation | async-start | bytes 10813440 | tf_op jit(solution)/shard_map/all_gather | solution.py:72
  145.7 570.3 %all-gather.7.cloned.1.call-start = ((), (), s32[]{:S(2)}) async-start(), calls=%async_computation.1 | async-start | bytes 8650752 | tf_op jit(solution)/shard_map/all_gather | solution.py:97
  149.1 152.2 %copy-start.5 = (f32[64,128]{1,0:T(8,128)}, f32[64,128]{1,0:T(8,128)S(1)}, u32[]{:S(2)}) copy-start(f32[64,128]{1,0:T(8,128)S(1)} %multiply_subtract_fusion.1) | copy-start | bytes 98308
  295.3 209.7 %copy-start.7 = (f32[5120]{0:T(1024)S(1)}, f32[5120]{0:T(1024)}, u32[]{:S(2)}) copy-start(f32[5120]{0:T(1024)} %param.16) | copy-start | bytes 61444
  498.8 7.0 copy-start.1
  505.8 3.4 copy-start.6
  505.8 3.6 copy-start.3
  505.8 3.6 copy-start.4
  514.0 208.3 %copy-start.2 = (bf16[4,256,160]{1,2,0:T(8,128)(2,1)S(1)}, bf16[4,256,160]{1,2,0:T(8,128)(2,1)}, u32[]{:S(2)}) copy-start(bf16[4,256,160]{1,2,0:T(8,128)(2,1)} %param.15) | copy-start | bytes 983044
Sparse Core Ops, SparseCore 0:
  11.6 131.6 all-reduce.2
  147.4 142.2 all-gather.8
  293.3 205.4 all-gather.4
  514.1 201.8 all-gather.6
where the time goes:
time: 738 us; the launch traced here: 730 us
  waiting for transfers between devices  674 us (91%)
  matrix products  19 us (3%)
  other arithmetic  15.1 us (2%)
  between operations  13.9 us (2%)
    all_gather x1, waiting for transfers between devices, body(): lax.all_gather(heads_out, 'tensor', axis=1, tiled=True)  202 us
    all_gather x1, waiting for transfers between devices, body(): lax.all_gather(hidden_in, 'tensor', axis=2, tiled=True).astype(jnp.float32)  198 us
    all_gather x1, waiting for transfers between devices, body(): lax.all_gather(new_down, 'tensor', axis=1, tiled=True)  141 us
    psum x1, waiting for transfers between devices, body(): down_total, up_total = lax.psum((down_part, up_part), 'group')  133 us
  transfers between devices with their start and end apart: 4, of which 4 were waited for; matrix products, arithmetic and copies ran while one was open for 2% of the time, Pallas kernels for 0%

commit v1 on v0

v1 whole, which is shorter than its diff:
```python
import jax
import jax.numpy as jnp
import numpy as np
from jax import lax
from jax.experimental import pallas as pl
from jax.experimental.pallas import tpu as pltpu
from jax.sharding import PartitionSpec as P

beta_first = 0.9
beta_second = 0.999
first_fix = 0.9999734386
second_fix = 0.095207851
learn_rate = 0.5
decay_rate = 0.01
adam_eps = 1e-08
norm_eps = 1e-06
rope_base = 1000000.0

MESH = pl.DeviceIdType.MESH
F32 = jnp.float32
BF16 = jnp.bfloat16
NZ = 16
NG = 16
FEAT = 160
WIDTH = 5120
HEAD = 128
ROWS = 128
STEPS = 4
CACHE = 8
RANK = 64
TOK = STEPS * ROWS
HQ = 4096


def adamw(param, first, second, grad):
    first_new = beta_first * first + (1.0 - beta_first) * grad
    second_new = beta_second * second + (1.0 - beta_second) * grad * grad
    first_hat = first_new / first_fix
    second_hat = second_new / second_fix
    return param - learn_rate * (first_hat / (jnp.sqrt(second_hat) + adam_eps) + decay_rate * param)


def aligned(start, size, multiple):
    return pl.ds(pl.multiple_of(start, multiple), size)


def kernel(
    hid, gain, gain_own, qw, qgain, ow, kv, pos, gdown, gup, dpar, dfir, dsec, upar, ufir, usec, freq,
    new_down, new_up, decoded,
    hidden_all, heads_all, w_raw, w_t, o_all, down_t, gd_buf, gu_buf, up_both, kv_buf, kv_f, kv_t, trig, query,
    pad_a, out_buf, local_sem, hx_s, hx_r, w_s, w_r, hcw_s, hcw_r, hcc_s, hcc_r, acw_s, acw_r, acc_s, acc_r,
    dcw_s, dcw_r, dcc_s, dcc_r, dx_s, dx_r, g_s, g_r, out_s, out_r,
):
    g = lax.axis_index("group")
    t = lax.axis_index("tensor")
    z = lax.div(t, 2)
    xh = lax.rem(t, 2)
    xo = 1 - xh
    partner = 2 * z + xo
    right = lax.rem(z + 1, NZ) * 2 + xh
    left = lax.rem(z + NZ - 1, NZ) * 2 + xh
    kvh = lax.div(t, 8)

    def zm(k):
        return lax.rem(z + 2 * NZ - k, NZ)

    def zp(k):
        return lax.rem(z + k, NZ)

    def remote(src, dst, s_sem, r_sem, axis, index):
        return pltpu.make_async_remote_copy(
            src_ref=src, dst_ref=dst, send_sem=s_sem, recv_sem=r_sem,
            device_id={axis: index}, device_id_type=MESH,
        )

    own_q = pltpu.make_async_copy(qw, w_raw.at[xh], local_sem.at[0])
    own_o = pltpu.make_async_copy(ow, o_all.at[aligned(xh * FEAT, FEAT, 32)], local_sem.at[1])
    own_kv = pltpu.make_async_copy(
        kv.at[:, aligned(xh * ROWS, ROWS, 128), :, aligned(kvh * HEAD, HEAD, 128)], kv_buf, local_sem.at[2])
    own_q.start()
    own_kv.start()
    own_o.start()

    barrier = pltpu.get_barrier_semaphore()
    for peer in (partner, right, left):
        pl.semaphore_signal(barrier, inc=1, device_id={"tensor": peer}, device_id_type=MESH)

    @pl.loop(1, NG)
    def _(k):
        pl.semaphore_signal(barrier, inc=1, device_id={"group": lax.rem(g + k, NG)}, device_id_type=MESH)

    pl.semaphore_wait(barrier, 3 + NG - 1)

    def chunk(s):
        return pl.ds(s * ROWS, ROWS)

    def hx(s):
        return remote(
            hid.at[s, :, aligned(xo * ROWS, ROWS, 128)],
            hidden_all.at[aligned(z * 2 * FEAT + xh * FEAT, FEAT, 32), chunk(s)],
            hx_s.at[s], hx_r.at[s], "tensor", partner)

    def hx_in(s):
        return remote(
            hid.at[s, :, aligned(xo * ROWS, ROWS, 128)],
            hidden_all.at[aligned(z * 2 * FEAT + xo * FEAT, FEAT, 32), chunk(s)],
            hx_s.at[s], hx_r.at[s], "tensor", partner)

    for s in range(STEPS):
        hx(s).start()

    def grad_copies(k):
        peer = lax.rem(g + k, NG)
        return (remote(gdown.at[0], gd_buf.at[k], g_s.at[0, k], g_r.at[0], "group", peer),
                remote(gup.at[0], gu_buf.at[k], g_s.at[1, k], g_r.at[1], "group", peer))

    @pl.loop(1, NG)
    def _(k):
        for copy in grad_copies(k):
            copy.start()

    for s in range(STEPS):
        hidden_all[aligned(z * 2 * FEAT + xh * FEAT, FEAT, 32), chunk(s)] = hid[s, :, aligned(xh * ROWS, ROWS, 128)]

    def ring(buf, size, k, s, forward, sems, sent):
        cw_s, cw_r, cc_s, cc_r = sems
        back = 1 if sent else 0
        if forward:
            source, s_sem, r_sem, peer = zm(k - back), cw_s.at[k - 1, s], cw_r.at[k - 1, s], right
        else:
            source, s_sem, r_sem, peer = zp(k - back), cc_s.at[k - 1, s], cc_r.at[k - 1, s], left
        block = buf.at[aligned(source * size, size, 32), chunk(s)]
        return remote(block, block, s_sem, r_sem, "tensor", peer)

    hid_sems = (hcw_s, hcw_r, hcc_s, hcc_r)
    head_sems = (acw_s, acw_r, acc_s, acc_r)

    def has(k, s, forward):
        return k < 8 or (s < 2) == forward

    def ring_step(buf, size, k, sems):
        for s in range(STEPS):
            for forward in (True, False):
                if has(k, s, forward):
                    ring(buf, size, k, s, forward, sems, False).wait_recv()
                    if k < 8 and has(k + 1, s, forward):
                        ring(buf, size, k + 1, s, forward, sems, True).start()

    def ring_end(buf, size, sems):
        for k in range(1, 9):
            for s in range(STEPS):
                for forward in (True, False):
                    if has(k, s, forward):
                        ring(buf, size, k, s, forward, sems, True).wait_send()

    for s in range(STEPS):
        hx_in(s).wait_recv()
        ring(hidden_all, 2 * FEAT, 1, s, True, hid_sems, True).start()
        ring(hidden_all, 2 * FEAT, 1, s, False, hid_sems, True).start()

    send_q = remote(qw, w_raw.at[xh], w_s.at[0], w_r.at[0], "tensor", partner)
    recv_q = remote(qw, w_raw.at[xo], w_s.at[0], w_r.at[0], "tensor", partner)
    send_o = remote(ow, o_all.at[aligned(xh * FEAT, FEAT, 32)], w_s.at[1], w_r.at[1], "tensor", partner)
    recv_o = remote(ow, o_all.at[aligned(xo * FEAT, FEAT, 32)], w_s.at[1], w_r.at[1], "tensor", partner)
    up_own = up_both.at[:, aligned(xh * HEAD, HEAD, 128)]
    up_other = up_both.at[:, aligned(xo * HEAD, HEAD, 128)]
    send_u = remote(up_own, up_own, w_s.at[2], w_r.at[2], "tensor", partner)
    recv_u = remote(up_other, up_other, w_s.at[2], w_r.at[2], "tensor", partner)
    send_q.start()
    send_o.start()

    def down_rows(zi, x):
        return down_t.at[aligned((2 * zi + x) * FEAT, FEAT, 32)]

    def down_ring(k, forward, sent):
        back = 1 if sent else 0
        if forward:
            source, sems, peer = zm(k - back), (dcw_s.at[k - 1], dcw_r.at[k - 1]), right
        else:
            source, sems, peer = zp(k - back), (dcc_s.at[k - 1], dcc_r.at[k - 1]), left
        block = down_rows(source, xh)
        return remote(block, block, *sems, "tensor", peer)

    def down_cross(j, sent):
        block = down_rows(zm(j) if j <= 8 else zp(j - 8), xh if sent else xo)
        return remote(block, block, dx_s.at[j], dx_r.at[j], "tensor", partner)

    def down_step(k):
        for forward in (True, False):
            if k < 8 or forward:
                down_ring(k, forward, False).wait_recv()
                if k < 7 or (forward and k < 8):
                    down_ring(k + 1, forward, True).start()
                down_cross(k if forward else 8 + k, True).start()

    def do_trig():
        for s in range(STEPS):
            angle = pos[s : s + 1, aligned(xh * ROWS, ROWS, 128)].astype(F32) * freq[...]
            trig[0, :, s * ROWS : (s + 1) * ROWS] = jnp.cos(angle)
            trig[1, :, s * ROWS : (s + 1) * ROWS] = jnp.sin(angle)

    def do_kv():
        own_kv.wait()
        for i in range(2):
            kv_f[...] = kv_buf[i].astype(F32)
            for c in range(CACHE):
                kv_t[i, c] = kv_f[:, c, :].T

    def do_w(x):
        @pl.loop(0, WIDTH // 128)
        def _(c):
            rows = aligned(c * 128, 128, 128)
            block = w_raw[x, rows, :].astype(F32).T * gain[pl.ds(c, 1), :]
            w_t[aligned(x * HEAD, HEAD, 128), rows] = block.astype(BF16)

    def do_adam():
        every = pl.ds(1, NG - 1)
        pltpu.make_async_copy(gd_buf.at[every], gd_buf.at[every], g_r.at[0]).wait()
        pltpu.make_async_copy(gu_buf.at[every], gu_buf.at[every], g_r.at[1]).wait()
        down_sum = gdown[0].astype(F32)
        up_sum = gup[0].astype(F32)
        for k in range(1, NG):
            down_sum += gd_buf[k].astype(F32)
            up_sum += gu_buf[k].astype(F32)
        down = adamw(dpar[...], dfir[...], dsec[...], down_sum)
        up = adamw(upar[...], ufir[...], usec[...], up_sum)
        new_down[...] = down
        new_up[...] = up
        up_both[:, aligned(xh * HEAD, HEAD, 128)] = up
        send_u.start()
        scaled = down * gain_own[...]
        hi = scaled.astype(BF16).astype(F32)
        pad_a[...] = jnp.zeros_like(pad_a)
        pad_a[:RANK, :FEAT] = hi
        pad_a[RANK:, :FEAT] = scaled - hi
        down_t[aligned((2 * z + xh) * FEAT, FEAT, 32), :] = pad_a[...].T[:FEAT, :].astype(BF16)
        down_ring(1, True, True).start()
        down_ring(1, False, True).start()
        down_cross(0, True).start()

    lag = 2
    for k in range(1, 9):
        ring_step(hidden_all, 2 * FEAT, k, hid_sems)
        if k > lag:
            down_step(k - lag)
        if k == 1:
            do_trig()
        elif k == 2:
            do_adam()
        elif k == 3:
            do_kv()
        elif k == 4:
            own_q.wait()
            do_w(xh)
        elif k == 6:
            recv_q.wait_recv()
            do_w(xo)

    def sum_squares(i, total):
        part = hidden_all[aligned(i * 64, 64, 64), :].astype(F32)
        return total + jnp.sum((part * part).reshape(8, 8, TOK), axis=0)

    square = lax.fori_loop(0, WIDTH // 64, sum_squares, jnp.zeros((8, TOK), F32))
    inverse = lax.rsqrt(jnp.sum(square, axis=0, keepdims=True) * (1.0 / WIDTH) + norm_eps)

    for k in range(9 - lag, 9):
        down_step(k)

    q_both = query.at[pl.ds(0, 2 * HEAD)]
    q_both[...] = jnp.zeros((2 * HEAD, TOK), F32)

    @pl.loop(0, WIDTH // 1024)
    def _(c):
        part = aligned(c * 1024, 1024, 1024)
        q_both[...] += jnp.dot(w_t[:, part], hidden_all[part, :], preferred_element_type=F32)

    for j in range(16):
        down_cross(j, False).wait_recv()

    def low_rank(c, total):
        part = aligned(c * 1024, 1024, 1024)
        return total + lax.dot_general(
            down_t[part, :], hidden_all[part, :], (((0,), (0,)), ((), ())), preferred_element_type=F32)

    low = lax.fori_loop(0, WIDTH // 1024, low_rank, jnp.zeros((2 * RANK, TOK), F32))
    low = low[:RANK] + low[RANK:]
    recv_u.wait_recv()
    delta = lax.dot_general(
        up_both[...], low, (((0,), (0,)), ((), ())),
        precision=lax.Precision.HIGHEST, preferred_element_type=F32)
    q_both[...] = (q_both[...] + delta * float(1.0 / np.sqrt(RANK * WIDTH))) * inverse

    qgain_col = jnp.broadcast_to(qgain[...], (HEAD, HEAD)).T
    half = HEAD // 2
    for x in range(2):
        for s in range(STEPS):
            lanes = slice(s * ROWS, (s + 1) * ROWS)
            q = query[x * HEAD : (x + 1) * HEAD, lanes]
            q = q * lax.rsqrt(jnp.sum(q * q, axis=0, keepdims=True) * (1.0 / HEAD) + norm_eps) * qgain_col
            cosine, sine = trig[0, :, lanes], trig[1, :, lanes]
            first, second = q[:half], q[half:]
            rotated = jnp.concatenate(
                [first * cosine - second * sine, second * cosine + first * sine], axis=0)
            rotated = rotated.astype(BF16).astype(F32)
            scores = jnp.concatenate(
                [jnp.sum(rotated * kv_t[0, c], axis=0, keepdims=True) for c in range(CACHE)], axis=0)
            scores = scores * float(1.0 / np.sqrt(HEAD))
            expo = jnp.exp(scores - jnp.max(scores, axis=0, keepdims=True))
            weights = (expo / jnp.sum(expo, axis=0, keepdims=True)).astype(BF16).astype(F32)
            total = weights[0:1] * kv_t[1, 0]
            for c in range(1, CACHE):
                total += weights[c : c + 1] * kv_t[1, c]
            heads_all[aligned(z * 2 * HEAD + x * HEAD, HEAD, 128), lanes] = total.astype(BF16)
    for s in range(STEPS):
        ring(heads_all, 2 * HEAD, 1, s, True, head_sems, True).start()
        ring(heads_all, 2 * HEAD, 1, s, False, head_sems, True).start()

    for k in range(1, 9):
        ring_step(heads_all, 2 * HEAD, k, head_sems)

    own_o.wait()
    recv_o.wait_recv()
    query[...] = hidden_all[aligned(z * 2 * FEAT, 2 * FEAT, 32), :].astype(F32)

    @pl.loop(0, HQ // 1024)
    def _(c):
        part = aligned(c * 1024, 1024, 1024)
        query[...] += jnp.dot(o_all[:, part], heads_all[part, :], preferred_element_type=F32)

    def out_copy(s, x):
        return remote(
            out_buf.at[s], decoded.at[s, :, aligned(x * ROWS, ROWS, 128)],
            out_s.at[s], out_r.at[s], "tensor", partner)

    for s in range(STEPS):
        lanes = slice(s * ROWS, (s + 1) * ROWS)
        out_buf[s] = query[aligned(xo * FEAT, FEAT, 32), lanes].astype(BF16)
        out_copy(s, xh).start()
        decoded[s, :, aligned(xh * ROWS, ROWS, 128)] = query[aligned(xh * FEAT, FEAT, 32), lanes].astype(BF16)

    ring_end(hidden_all, 2 * FEAT, hid_sems)
    ring_end(heads_all, 2 * HEAD, head_sems)
    for k in range(1, 9):
        down_ring(k, True, True).wait_send()
        if k < 8:
            down_ring(k, False, True).wait_send()
    for j in range(16):
        down_cross(j, True).wait_send()
    for s in range(STEPS):
        hx(s).wait_send()
    for copy in (send_q, send_o, send_u):
        copy.wait_send()

    @pl.loop(1, NG)
    def _(k):
        for copy in grad_copies(k):
            copy.wait_send()

    for s in range(STEPS):
        out_copy(s, xh).wait_send()
        out_copy(s, xo).wait_recv()


def body(hidden_in, norm_gain, q_weight, q_gain, o_weight, kv_cache, positions, grad_down, grad_up, *factors):
    t = lax.axis_index("tensor")
    freq = np.float32(rope_base) ** (-2.0 * np.arange(HEAD // 2, dtype=np.float32) / HEAD)
    freq = jnp.asarray(np.broadcast_to(freq.astype(np.float32)[:, None], (HEAD // 2, ROWS)))
    gain_own = lax.dynamic_slice(norm_gain, (t * FEAT,), (FEAT,)).reshape(1, FEAT)
    vmem = pl.BlockSpec(memory_space=pltpu.VMEM)
    anywhere = pl.BlockSpec(memory_space=pl.ANY)
    dma = pltpu.SemaphoreType.DMA
    new_down, new_up, decoded = pl.pallas_call(
        kernel,
        out_shape=(
            jax.ShapeDtypeStruct((RANK, FEAT), F32),
            jax.ShapeDtypeStruct((RANK, HEAD), F32),
            jax.ShapeDtypeStruct((STEPS, FEAT, 2 * ROWS), BF16),
        ),
        in_specs=[vmem, vmem, vmem, anywhere, vmem, anywhere, anywhere] + [vmem] * 10,
        out_specs=(vmem, vmem, vmem),
        scratch_shapes=[
            pltpu.VMEM((WIDTH, TOK), BF16),
            pltpu.VMEM((HQ, TOK), BF16),
            pltpu.VMEM((2, WIDTH, HEAD), BF16),
            pltpu.VMEM((2 * HEAD, WIDTH), BF16),
            pltpu.VMEM((2 * FEAT, HQ), BF16),
            pltpu.VMEM((WIDTH, 2 * RANK), BF16),
            pltpu.VMEM((NG, RANK, FEAT), BF16),
            pltpu.VMEM((NG, RANK, HEAD), BF16),
            pltpu.VMEM((RANK, 2 * HEAD), F32),
            pltpu.VMEM((2, ROWS, CACHE, HEAD), BF16),
            pltpu.VMEM((ROWS, CACHE, HEAD), F32),
            pltpu.VMEM((2, CACHE, HEAD, ROWS), F32),
            pltpu.VMEM((2, HEAD // 2, TOK), F32),
            pltpu.VMEM((2 * FEAT, TOK), F32),
            pltpu.VMEM((2 * RANK, 256), F32),
            pltpu.VMEM((STEPS, FEAT, ROWS), BF16),
            dma((3,)),
            dma((STEPS,)), dma((STEPS,)),
            dma((3,)), dma((3,)),
            dma((8, STEPS)), dma((8, STEPS)), dma((8, STEPS)), dma((8, STEPS)),
            dma((8, STEPS)), dma((8, STEPS)), dma((8, STEPS)), dma((8, STEPS)),
            dma((8,)), dma((8,)), dma((8,)), dma((8,)),
            dma((16,)), dma((16,)),
            dma((2, NG)), dma((2,)),
            dma((STEPS,)), dma((STEPS,)),
        ],
        compiler_params=pltpu.CompilerParams(
            collective_id=0, has_side_effects=True, vmem_limit_bytes=56 * 1024 * 1024),
        cost_estimate=pl.CostEstimate(flops=3_000_000_000, bytes_accessed=10_000_000, transcendentals=100_000),
    )(
        jnp.transpose(hidden_in, (0, 2, 1)), norm_gain.reshape(WIDTH // 128, 128), gain_own, q_weight,
        q_gain.reshape(1, HEAD), jnp.transpose(o_weight), kv_cache, positions, grad_down, grad_up,
        *factors, freq,
    )
    return new_down, new_up, jnp.transpose(decoded, (0, 2, 1))


def solution(mesh):
    in_specs = (
        P(None, "group", "tensor"),
        P(),
        P(None, "tensor"),
        P(),
        P(None, "tensor"),
        P(None, "group", None, None),
        P(None, "group"),
        P("group", None, "tensor"),
        P("group", None, "tensor"),
        P(None, "tensor"),
        P(None, "tensor"),
        P(None, "tensor"),
        P(None, "tensor"),
        P(None, "tensor"),
        P(None, "tensor"),
    )
    out_specs = (P(None, "tensor"), P(None, "tensor"), P(None, "group", "tensor"))
    return jax.shard_map(body, mesh=mesh, in_specs=in_specs, out_specs=out_specs, check_vma=False)
```

time: 738 us -> 166 us (0.22); the launches traced: 730 us -> 166 us
  waiting for transfers between devices: 674 us -> 0 us
  Pallas kernels: 0 us -> 158 us
  matrix products: 19 us -> 0 us
  other arithmetic: 15.1 us -> 0 us
  between operations: 13.9 us -> 0.64 us
    all_gather x3 -> x0, waiting for transfers between devices: 540 us -> none  [the longest x1 202 us: body(): lax.all_gather(heads_out, 'tensor', axis=1, tiled=True)]
    pallas_call x0 -> x1, Pallas kernels: none -> 158 us  [body(): pl.pallas_call(kernel, out_shape=(jax.ShapeDtypeStruct((RANK, FEAT), F32)...]
    psum x1 -> x0, waiting for transfers between devices: 133 us -> none  [body(): down_total, up_total = lax.psum((down_part, up_part), 'group')]
    dot_general x4 -> x0, matrix products: 17.2 us -> none  [the longest x1 6.28 us: body(): jnp.dot(lax.all_gather(heads_out, 'tensor', axis=1, tiled=True), o_weight...]
  transfers between devices with their start and end apart: 4 -> 0, of which waited for: 4 -> 0; matrix products, arithmetic and copies ran while one was open for 2% -> 0% of each run, Pallas kernels for 0% -> 0%
where the time goes in v1:
time: 166 us
  Pallas kernels  158 us (95%)
  local copies, waits for them, and re-layouts  7.25 us (4%)
    pallas_call x1, Pallas kernels, body(): pl.pallas_call(kernel, out_shape=(jax.ShapeDtypeStruct((RANK, FEAT), F32)...  158 us
    unnamed x3, local copies, waits for them, and re-layouts  4.56 us

profile of v1, /device:TPU:1, one launch (start us, length us, event | category | flops | bytes accessed | tf_op | source)
XLA Modules:
  0.0 165.8 jit_solution(13137812462468119340)
XLA Ops:
  0.6 1.3 dynamic_slice.3
  2.0 1.3 jit_solution_.3.freq
  3.3 157.9 %shard_map.175 = (f32[64,160]{1,0:T(8,128)}, f32[64,128]{1,0:T(8,128)}, bf16[4,160,256]{2,1,0:T(8,128)(2,1)}) custom-call(bf16[4,160,256]{2,1,0:T(8,128)(2,1)} %bitcast.10, f32[40,128]{1,0:T(8,128)} %bitcast.8, f32[1,160]{1,0:T(1,128)} %bitcast.7, bf16[5120,128]{1,0:T(8,128)(2,1)} %qw.1, f32[1,128]{1,0:T(1,128)} %bitcast.11, bf16[160,4096]{1,0:T(8,128)(2,1)} %bitcast.9, ...), custom_call_target="tpu_custom_call" | custom-call | flops 3000000000 | bytes 10000000 | tf_op jit(solution)/shard_map/pallas_call | solution.py:372
  161.3 1.5 copy.22
  162.7 1.4 copy.23
  164.1 1.7 %copy.24 = bf16[4,256,160]{1,2,0:T(8,128)(2,1)} copy(bf16[4,256,160]{1,2,0:T(8,128)(2,1)} %bitcast.6) | data formatting | bytes 655360

commit v2 on v1

v2 whole, which is shorter than its diff:
```python
import jax
import jax.numpy as jnp
import numpy as np
from jax import lax
from jax.experimental import pallas as pl
from jax.experimental.pallas import tpu as pltpu
from jax.sharding import PartitionSpec as P

beta_first = 0.9
beta_second = 0.999
first_fix = 0.9999734386
second_fix = 0.095207851
learn_rate = 0.5
decay_rate = 0.01
adam_eps = 1e-08
norm_eps = 1e-06
rope_base = 1000000.0

MESH = pl.DeviceIdType.MESH
F32 = jnp.float32
BF16 = jnp.bfloat16
NZ = 16
NG = 16
FEAT = 160
WIDTH = 5120
HEAD = 128
ROWS = 128
STEPS = 4
CACHE = 8
RANK = 64
TOK = STEPS * ROWS
HQ = 4096


def adamw(param, first, second, grad):
    first_new = beta_first * first + (1.0 - beta_first) * grad
    second_new = beta_second * second + (1.0 - beta_second) * grad * grad
    first_hat = first_new / first_fix
    second_hat = second_new / second_fix
    return param - learn_rate * (first_hat / (jnp.sqrt(second_hat) + adam_eps) + decay_rate * param)


def aligned(start, size, multiple):
    return pl.ds(pl.multiple_of(start, multiple), size)


def kernel(
    hid, gain, qw, qgain, ow, kv, pos, gdown, gup, dpar, dfir, dsec, upar, ufir, usec, freq_hbm,
    new_down, new_up, decoded,
    hidden_all, heads_all, w_raw, o_all, down_t, gd_buf, gu_buf, up_both, kv_buf, kv_f, kv_t, trig, query, low,
    square, gain_col, freq, pad_a, out_buf,
    local_sem, hx_s, hx_r, w_s, w_r, hcw_s, hcw_r, hcc_s, hcc_r, acw_s, acw_r, acc_s, acc_r,
    da_s, da_r, dx_s, dx_r, db_s, db_r, g_s, g_r, out_s, out_r,
):
    g = lax.axis_index("group")
    t = lax.axis_index("tensor")
    z = lax.div(t, 2)
    xh = lax.rem(t, 2)
    xo = 1 - xh
    core = lax.rem(g, 2)
    sibling = g + 1 - 2 * core
    partner = 2 * z + xo
    right = lax.rem(z + 1, NZ) * 2 + xh
    left = lax.rem(z + NZ - 1, NZ) * 2 + xh
    kvh = lax.div(t, 8)

    def zm(k):
        return lax.rem(z + 2 * NZ - k, NZ)

    def zp(k):
        return lax.rem(z + k, NZ)

    def remote(src, dst, s_sem, r_sem, axis, index):
        return pltpu.make_async_remote_copy(
            src_ref=src, dst_ref=dst, send_sem=s_sem, recv_sem=r_sem,
            device_id={axis: index}, device_id_type=MESH,
        )

    def lanes(s):
        return pl.ds(s * ROWS, ROWS)

    own_q = pltpu.make_async_copy(qw, w_raw.at[xh], local_sem.at[0])
    own_o = pltpu.make_async_copy(ow, o_all.at[aligned(xh * FEAT, FEAT, 32)], local_sem.at[1])
    own_kv = pltpu.make_async_copy(
        kv.at[:, aligned(xh * ROWS, ROWS, 128), :, aligned(kvh * HEAD, HEAD, 128)], kv_buf, local_sem.at[2])
    own_freq = pltpu.make_async_copy(freq_hbm, freq, local_sem.at[3])
    own_freq.start()
    own_kv.start()
    own_q.start()
    own_o.start()

    barrier = pltpu.get_barrier_semaphore()
    pl.semaphore_signal(barrier, inc=1, device_id={"tensor": partner}, device_id_type=MESH)

    @pl.loop(1, NG)
    def _(k):
        pl.semaphore_signal(barrier, inc=1, device_id={"tensor": 2 * zp(k) + xh}, device_id_type=MESH)
        pl.semaphore_signal(barrier, inc=1, device_id={"group": lax.rem(g + k, NG)}, device_id_type=MESH)

    for s in range(STEPS):
        hidden_all[aligned((2 * z + xh) * FEAT, FEAT, 32), lanes(s)] = hid[s, :, aligned(xh * ROWS, ROWS, 128)]

    pl.semaphore_wait(barrier, 1 + 2 * (NG - 1))

    def hx(s, sent):
        return remote(
            hid.at[s, :, aligned(xo * ROWS, ROWS, 128)],
            hidden_all.at[aligned((2 * z + (xh if sent else xo)) * FEAT, FEAT, 32), lanes(s)],
            hx_s.at[s], hx_r.at[s], "tensor", partner)

    def hidden_chunk(zi, j):
        x = xh if j < 2 else xo
        return hidden_all.at[aligned((2 * zi + x) * FEAT, FEAT, 32), pl.ds((j % 2) * 2 * ROWS, 2 * ROWS)]

    def head_chunk(zi, j):
        return heads_all.at[aligned(zi * 2 * HEAD, 2 * HEAD, 256), lanes(j)]

    def ring(chunk, k, j, forward, sems, sent):
        cw_s, cw_r, cc_s, cc_r = sems
        back = 1 if sent else 0
        if forward:
            source, s_sem, r_sem, peer = zm(k - back), cw_s.at[k - 1, j], cw_r.at[k - 1, j], right
        else:
            source, s_sem, r_sem, peer = zp(k - back), cc_s.at[k - 1, j], cc_r.at[k - 1, j], left
        block = chunk(source, j)
        return remote(block, block, s_sem, r_sem, "tensor", peer)

    hid_sems = (hcw_s, hcw_r, hcc_s, hcc_r)
    head_sems = (acw_s, acw_r, acc_s, acc_r)

    def has(k, j, forward):
        return k < 8 or (j % 2 == 0) == forward

    def ring_start(chunk, j, sems):
        ring(chunk, 1, j, True, sems, True).start()
        ring(chunk, 1, j, False, sems, True).start()

    def ring_run(chunk, sems, work):
        for k in range(1, 9):
            for j in range(4):
                for forward in (True, False):
                    if has(k, j, forward):
                        ring(chunk, k, j, forward, sems, False).wait_recv()
                        if k < 8 and has(k + 1, j, forward):
                            ring(chunk, k + 1, j, forward, sems, True).start()
                for unit in work.get((k, j), ()):
                    unit()

    def ring_end(chunk, sems):
        for k in range(1, 9):
            for j in range(4):
                for forward in (True, False):
                    if has(k, j, forward):
                        ring(chunk, k, j, forward, sems, True).wait_send()

    def grad_copies(k):
        peer = lax.rem(g + k, NG)
        return (remote(gdown.at[0], gd_buf.at[k], g_s.at[0, k], g_r.at[0], "group", peer),
                remote(gup.at[0], gu_buf.at[k], g_s.at[1, k], g_r.at[1], "group", peer))

    for s in range(STEPS):
        hx(s, True).start()
    ring_start(hidden_chunk, 0, hid_sems)
    ring_start(hidden_chunk, 1, hid_sems)

    @pl.loop(1, NG)
    def _(k):
        for copy in grad_copies(k):
            copy.start()

    def q_half(x, c):
        return w_raw.at[x, aligned(c * (WIDTH // 2), WIDTH // 2, 32)]

    def o_half(x, c):
        return o_all.at[aligned(x * FEAT, FEAT, 32), aligned(c * (HQ // 2), HQ // 2, 128)]

    def send_q(sent):
        return remote(qw.at[aligned(core * (WIDTH // 2), WIDTH // 2, 32)], q_half(xh if sent else xo, core),
                      w_s.at[0], w_r.at[0], "tensor", partner)

    def share_q(sent):
        return remote(q_half(xo, core), q_half(xo, core if sent else 1 - core),
                      w_s.at[1], w_r.at[1], "group", sibling)

    def send_o(sent):
        return remote(ow.at[:, aligned(core * (HQ // 2), HQ // 2, 128)], o_half(xh if sent else xo, core),
                      w_s.at[2], w_r.at[2], "tensor", partner)

    def share_o(sent):
        return remote(o_half(xo, core), o_half(xo, core if sent else 1 - core),
                      w_s.at[3], w_r.at[3], "group", sibling)

    def send_u(sent):
        block = up_both.at[:, aligned((xh if sent else xo) * HEAD, HEAD, 128)]
        return remote(block, block, w_s.at[4], w_r.at[4], "tensor", partner)

    send_q(True).start()
    for s in range(STEPS):
        hx(s, False).wait_recv()
        if s % 2:
            ring_start(hidden_chunk, 2 + s // 2, hid_sems)

    def down_rows(zi, x):
        return down_t.at[aligned((2 * zi + x) * FEAT, FEAT, 32)]

    def down_along(k):
        return remote(down_rows(g, xh), down_rows(g, xh), da_s.at[k], da_r.at[0], "tensor", 2 * zp(k) + xh)

    def down_cross(sent):
        block = down_rows(g, xh if sent else xo)
        return remote(block, block, dx_s.at[0], dx_r.at[0], "tensor", partner)

    def down_share(k, sent):
        owner = g if sent else lax.rem(g + NG - k, NG)
        block = down_t.at[aligned(owner * 2 * FEAT, 2 * FEAT, 32)]
        return remote(block, block, db_s.at[k], db_r.at[k], "group", lax.rem(g + k, NG))

    def down_first_part():
        @pl.when(z != g)
        def _():
            down_along(1).wait_recv()

        down_cross(True).start()

    def down_second_part():
        down_cross(False).wait_recv()

        @pl.loop(1, NG)
        def _(k):
            down_share(k, True).start()

    def down_wait():
        @pl.loop(1, NG)
        def _(k):
            down_share(k, False).wait_recv()

    def do_gain(i):
        for c in range(8 * i, 8 * i + 8):
            gain_col[c * 128 : (c + 1) * 128, :] = jnp.broadcast_to(gain[c : c + 1, :], (128, 128)).T

    def do_trig(s):
        angle = pos[s : s + 1, aligned(xh * ROWS, ROWS, 128)].astype(F32) * freq[...]
        trig[0, :, lanes(s)] = jnp.cos(angle)
        trig[1, :, lanes(s)] = jnp.sin(angle)

    def do_kv(i, j):
        if j == 0:
            kv_f[...] = kv_buf[i].astype(F32)
        for c in range(4 * j, 4 * j + 4):
            kv_t[i, c] = kv_f[:, c, :].T

    def do_w(x, i):
        part = pl.ds(i * 1024, 1024)
        w_raw[x, part, :] = (w_raw[x, part, :].astype(F32) * gain_col[part, :]).astype(BF16)

    def do_sums():
        every = pl.ds(1, NG - 1)
        pltpu.make_async_copy(gd_buf.at[every], gd_buf.at[every], g_r.at[0]).wait()
        pltpu.make_async_copy(gu_buf.at[every], gu_buf.at[every], g_r.at[1]).wait()
        down_sum = gdown[0].astype(F32)
        up_sum = gup[0].astype(F32)
        for k in range(1, NG):
            down_sum += gd_buf[k].astype(F32)
            up_sum += gu_buf[k].astype(F32)
        down = adamw(dpar[...], dfir[...], dsec[...], down_sum)
        up = adamw(upar[...], ufir[...], usec[...], up_sum)
        new_down[...] = down
        new_up[...] = up
        up_both[:, aligned(xh * HEAD, HEAD, 128)] = up
        send_u(True).start()

        @pl.when(z == g)
        def _():
            pad_a[...] = jnp.zeros_like(pad_a)
            pad_a[:RANK, :FEAT] = down
            pad_a[RANK:, :FEAT] = down
            scaled = pad_a[...].T[:FEAT, :] * gain_col[aligned(t * FEAT, FEAT, 32), :]
            hi = scaled.astype(BF16).astype(F32)
            lane = lax.broadcasted_iota(jnp.int32, (FEAT, 2 * RANK), 1)
            down_t[aligned((2 * g + xh) * FEAT, FEAT, 32), :] = jnp.where(lane < RANK, hi, scaled - hi).astype(BF16)

            @pl.loop(1, NZ)
            def _(k):
                down_along(k).start()

    q_both = query.at[pl.ds(0, 2 * HEAD)]
    across = (((0,), (0,)), ((), ()))

    def q_block(zi):
        rows = aligned(zi * 2 * FEAT, 2 * FEAT, 64)
        block = hidden_all[rows, :]
        for x in range(2):
            query[x * HEAD : (x + 1) * HEAD, :] += lax.dot_general(
                w_raw[x, rows, :], block, across, preferred_element_type=F32)
        wide = block.astype(F32)
        square[...] += jnp.sum((wide * wide).reshape(2 * FEAT // 8, 8, TOK), axis=0)

    def low_block(zi):
        rows = aligned(zi * 2 * FEAT, 2 * FEAT, 64)
        low[...] += lax.dot_general(down_t[rows, :], hidden_all[rows, :], across, preferred_element_type=F32)

    def start_sums():
        q_both[...] = jnp.zeros((2 * HEAD, TOK), F32)
        low[...] = jnp.zeros_like(low)
        square[...] = jnp.zeros_like(square)

    arrived = [zm(0)] + [f(k) for k in range(1, 8) for f in (zm, zp)]
    work = {
        (1, 0): [lambda: do_gain(0), lambda: do_gain(1)],
        (1, 1): [lambda: do_gain(2), lambda: do_gain(3)],
        (1, 2): [lambda: do_gain(4), own_freq.wait, lambda: do_trig(0)],
        (1, 3): [lambda: do_trig(1)],
        (2, 0): [do_sums],
        (2, 1): [lambda: do_trig(2)],
        (2, 2): [lambda: do_trig(3)],
        (2, 3): [own_kv.wait, lambda: do_kv(0, 0)],
        (3, 0): [lambda: do_kv(0, 1)],
        (3, 1): [lambda: do_kv(1, 0)],
        (3, 2): [lambda: do_kv(1, 1)],
        (3, 3): [own_q.wait, lambda: do_w(xh, 0)],
        (4, 0): [down_first_part, lambda: do_w(xh, 1)],
        (4, 1): [send_q(False).wait_recv, share_q(True).start],
        (4, 2): [lambda: do_w(xh, 2), lambda: do_w(xh, 3)],
        (4, 3): [lambda: do_w(xh, 4), start_sums],
        (5, 0): [down_second_part, send_o(True).start],
        (5, 1): [share_q(False).wait_recv, share_q(True).wait_send, lambda: do_w(xo, 0)],
        (5, 2): [lambda: do_w(xo, 1), lambda: do_w(xo, 2)],
        (5, 3): [lambda: do_w(xo, 3), lambda: do_w(xo, 4)],
    }
    for i in range(8):
        work.setdefault((6, i // 2), []).append(lambda zi=arrived[i]: q_block(zi))
    for i in range(8, 13):
        work.setdefault((7, min(i - 8, 3)), []).append(lambda zi=arrived[i]: q_block(zi))
    work[(8, 0)] = [lambda zi=arrived[13]: q_block(zi), lambda zi=arrived[14]: q_block(zi)]
    work[(8, 1)] = [down_wait] + [lambda zi=zi: low_block(zi) for zi in arrived[:5]]
    work[(8, 2)] = [lambda zi=zi: low_block(zi) for zi in arrived[5:10]]
    ring_run(hidden_chunk, hid_sems, work)
    for zi in arrived[10:] + [zm(8)]:
        low_block(zi)
    q_block(zm(8))

    inverse = lax.rsqrt(jnp.sum(square[...], axis=0, keepdims=True) * (1.0 / WIDTH) + norm_eps)
    send_u(False).wait_recv()
    delta = lax.dot_general(
        up_both[...], low[:RANK, :] + low[RANK:, :], across,
        precision=lax.Precision.HIGHEST, preferred_element_type=F32)
    q_both[...] = (q_both[...] + delta * float(1.0 / np.sqrt(RANK * WIDTH))) * inverse

    qgain_col = jnp.broadcast_to(qgain[...], (HEAD, HEAD)).T
    half = HEAD // 2
    for s in range(STEPS):
        for x in range(2):
            q = query[x * HEAD : (x + 1) * HEAD, lanes(s)]
            q = q * lax.rsqrt(jnp.sum(q * q, axis=0, keepdims=True) * (1.0 / HEAD) + norm_eps) * qgain_col
            cosine, sine = trig[0, :, lanes(s)], trig[1, :, lanes(s)]
            first, second = q[:half], q[half:]
            rotated = jnp.concatenate(
                [first * cosine - second * sine, second * cosine + first * sine], axis=0)
            rotated = rotated.astype(BF16).astype(F32)
            scores = jnp.concatenate(
                [jnp.sum(rotated * kv_t[0, c], axis=0, keepdims=True) for c in range(CACHE)], axis=0)
            scores = scores * float(1.0 / np.sqrt(HEAD))
            expo = jnp.exp(scores - jnp.max(scores, axis=0, keepdims=True))
            weights = (expo / jnp.sum(expo, axis=0, keepdims=True)).astype(BF16).astype(F32)
            total = weights[0:1] * kv_t[1, 0]
            for c in range(1, CACHE):
                total += weights[c : c + 1] * kv_t[1, c]
            heads_all[aligned((2 * z + x) * HEAD, HEAD, 128), lanes(s)] = total.astype(BF16)
        ring_start(head_chunk, s, head_sems)

    def o_start():
        query[...] = hidden_all[aligned(z * 2 * FEAT, 2 * FEAT, 64), :].astype(F32)

    def o_block(zi):
        part = aligned(zi * 2 * HEAD, 2 * HEAD, 256)
        query[...] += jnp.dot(o_all[:, part], heads_all[part, :], preferred_element_type=F32)

    work = {
        (1, 0): [send_o(False).wait_recv, share_o(True).start],
        (1, 1): [o_start],
        (1, 3): [own_o.wait, share_o(False).wait_recv],
        (2, 3): [lambda: o_block(zm(0))],
    }
    for k in range(2, 9):
        work.setdefault((k, 0), []).append(lambda k=k: o_block(zm(k - 1)))
        work.setdefault((k, 1), []).append(lambda k=k: o_block(zp(k - 1)))
    ring_run(head_chunk, head_sems, work)
    o_block(zm(8))

    def out_copy(s, x):
        return remote(
            out_buf.at[s], decoded.at[s, :, aligned(x * ROWS, ROWS, 128)],
            out_s.at[s], out_r.at[s], "tensor", partner)

    for s in range(STEPS):
        out_buf[s] = query[aligned(xo * FEAT, FEAT, 32), lanes(s)].astype(BF16)
        out_copy(s, xh).start()
    for s in range(STEPS):
        decoded[s, :, aligned(xh * ROWS, ROWS, 128)] = query[aligned(xh * FEAT, FEAT, 32), lanes(s)].astype(BF16)

    ring_end(hidden_chunk, hid_sems)
    ring_end(head_chunk, head_sems)
    for s in range(STEPS):
        hx(s, True).wait_send()
    for copy in (send_q, send_o, share_o, send_u, down_cross):
        copy(True).wait_send()

    @pl.when(z == g)
    def _():
        @pl.loop(1, NZ)
        def _(k):
            down_along(k).wait_send()

    @pl.loop(1, NG)
    def _(k):
        for copy in grad_copies(k):
            copy.wait_send()
        down_share(k, True).wait_send()

    for s in range(STEPS):
        out_copy(s, xh).wait_send()
        out_copy(s, xo).wait_recv()


def body(hidden_in, norm_gain, q_weight, q_gain, o_weight, kv_cache, positions, grad_down, grad_up, *factors):
    freq = np.float32(rope_base) ** (-2.0 * np.arange(HEAD // 2, dtype=np.float32) / HEAD)
    freq = jnp.asarray(np.broadcast_to(freq.astype(np.float32)[:, None], (HEAD // 2, ROWS)))
    vmem = pl.BlockSpec(memory_space=pltpu.VMEM)
    anywhere = pl.BlockSpec(memory_space=pl.ANY)
    dma = pltpu.SemaphoreType.DMA
    new_down, new_up, decoded = pl.pallas_call(
        kernel,
        out_shape=(
            jax.ShapeDtypeStruct((RANK, FEAT), F32),
            jax.ShapeDtypeStruct((RANK, HEAD), F32),
            jax.ShapeDtypeStruct((STEPS, FEAT, 2 * ROWS), BF16),
        ),
        in_specs=[vmem, vmem, anywhere, vmem, anywhere, anywhere] + [vmem] * 9 + [anywhere],
        out_specs=(vmem, vmem, vmem),
        scratch_shapes=[
            pltpu.VMEM((WIDTH, TOK), BF16),
            pltpu.VMEM((HQ, TOK), BF16),
            pltpu.VMEM((2, WIDTH, HEAD), BF16),
            pltpu.VMEM((2 * FEAT, HQ), BF16),
            pltpu.VMEM((WIDTH, 2 * RANK), BF16),
            pltpu.VMEM((NG, RANK, FEAT), BF16),
            pltpu.VMEM((NG, RANK, HEAD), BF16),
            pltpu.VMEM((RANK, 2 * HEAD), F32),
            pltpu.VMEM((2, ROWS, CACHE, HEAD), BF16),
            pltpu.VMEM((ROWS, CACHE, HEAD), F32),
            pltpu.VMEM((2, CACHE, HEAD, ROWS), F32),
            pltpu.VMEM((2, HEAD // 2, TOK), F32),
            pltpu.VMEM((2 * FEAT, TOK), F32),
            pltpu.VMEM((2 * RANK, TOK), F32),
            pltpu.VMEM((8, TOK), F32),
            pltpu.VMEM((WIDTH, 128), F32),
            pltpu.VMEM((HEAD // 2, ROWS), F32),
            pltpu.VMEM((2 * RANK, 256), F32),
            pltpu.VMEM((STEPS, FEAT, ROWS), BF16),
            dma((4,)),
            dma((STEPS,)), dma((STEPS,)),
            dma((5,)), dma((5,)),
            dma((8, 4)), dma((8, 4)), dma((8, 4)), dma((8, 4)),
            dma((8, 4)), dma((8, 4)), dma((8, 4)), dma((8, 4)),
            dma((NZ,)), dma((1,)), dma((1,)), dma((1,)), dma((NG,)), dma((NG,)),
            dma((2, NG)), dma((2,)),
            dma((STEPS,)), dma((STEPS,)),
        ],
        compiler_params=pltpu.CompilerParams(
            collective_id=0, has_side_effects=True, vmem_limit_bytes=56 * 1024 * 1024),
        cost_estimate=pl.CostEstimate(flops=3_000_000_000, bytes_accessed=10_000_000, transcendentals=100_000),
    )(
        jnp.transpose(hidden_in, (0, 2, 1)), norm_gain.reshape(WIDTH // 128, 128), q_weight,
        q_gain.reshape(1, HEAD), jnp.transpose(o_weight), kv_cache, positions, grad_down, grad_up,
        *factors, freq,
    )
    return new_down, new_up, jnp.transpose(decoded, (0, 2, 1))


def solution(mesh):
    in_specs = (
        P(None, "group", "tensor"),
        P(),
        P(None, "tensor"),
        P(),
        P(None, "tensor"),
        P(None, "group", None, None),
        P(None, "group"),
        P("group", None, "tensor"),
        P("group", None, "tensor"),
        P(None, "tensor"),
        P(None, "tensor"),
        P(None, "tensor"),
        P(None, "tensor"),
        P(None, "tensor"),
        P(None, "tensor"),
    )
    out_specs = (P(None, "tensor"), P(None, "tensor"), P(None, "group", "tensor"))
    return jax.shard_map(body, mesh=mesh, in_specs=in_specs, out_specs=out_specs, check_vma=False)
```

time: 166 us -> 141 us (0.85)
  Pallas kernels: 158 us -> 134 us
    pallas_call x1, Pallas kernels: 158 us -> 134 us  [body(): pl.pallas_call(kernel, out_shape=(jax.ShapeDtypeStruct((RANK, FEAT), F32)...]
where the time goes in v2:
time: 141 us
  Pallas kernels  134 us (95%)
  local copies, waits for them, and re-layouts  5.91 us (4%)
    pallas_call x1, Pallas kernels, body(): pl.pallas_call(kernel, out_shape=(jax.ShapeDtypeStruct((RANK, FEAT), F32)...  134 us
    unnamed x3, local copies, waits for them, and re-layouts  4.56 us

profile of v2, /device:TPU:1, one launch (start us, length us, event | category | flops | bytes accessed | tf_op | source)
XLA Modules:
  0.0 140.7 jit_solution(9152635133997982347)
XLA Ops:
  0.6 1.3 jit_solution_.3.freq_hbm
  2.0 134.2 %shard_map.175 = (f32[64,160]{1,0:T(8,128)}, f32[64,128]{1,0:T(8,128)}, bf16[4,160,256]{2,1,0:T(8,128)(2,1)}) custom-call(bf16[4,160,256]{2,1,0:T(8,128)(2,1)} %bitcast.7, f32[40,128]{1,0:T(8,128)} %bitcast.8, bf16[5120,128]{1,0:T(8,128)(2,1)} %qw.1, f32[1,128]{1,0:T(1,128)} %bitcast.9, bf16[160,4096]{1,0:T(8,128)(2,1)} %bitcast.6, ...), custom_call_target="tpu_custom_call" | custom-call | flops 3000000000 | bytes 10000000 | tf_op jit(solution)/shard_map/pallas_call | solution.py:431
  136.1 1.5 %copy.22 = f32[64,160]{1,0:T(8,128)} copy(f32[64,160]{1,0:T(8,128)} %get-tuple-element.12) | data formatting | bytes 81920
  137.6 1.4 copy.23
  139.0 1.7 %copy.24 = bf16[4,256,160]{1,2,0:T(8,128)(2,1)} copy(bf16[4,256,160]{1,2,0:T(8,128)(2,1)} %bitcast.5) | data formatting | bytes 655360

commit v3 on v2

v3 whole, which is shorter than its diff:
```python
import jax
import jax.numpy as jnp
import numpy as np
from jax import lax
from jax.experimental import pallas as pl
from jax.experimental.pallas import tpu as pltpu
from jax.sharding import PartitionSpec as P

beta_first = 0.9
beta_second = 0.999
first_fix = 0.9999734386
second_fix = 0.095207851
learn_rate = 0.5
decay_rate = 0.01
adam_eps = 1e-08
norm_eps = 1e-06
rope_base = 1000000.0

MESH = pl.DeviceIdType.MESH
F32 = jnp.float32
BF16 = jnp.bfloat16
NZ = 16
NG = 16
FEAT = 160
WIDTH = 5120
HEAD = 128
ROWS = 128
STEPS = 4
CACHE = 8
RANK = 64
TOK = STEPS * ROWS
HQ = 4096
PIECES = 16


def adamw(param, first, second, grad):
    first_new = beta_first * first + (1.0 - beta_first) * grad
    second_new = beta_second * second + (1.0 - beta_second) * grad * grad
    first_hat = first_new / first_fix
    second_hat = second_new / second_fix
    return param - learn_rate * (first_hat / (jnp.sqrt(second_hat) + adam_eps) + decay_rate * param)


def aligned(start, size, multiple):
    return pl.ds(pl.multiple_of(start, multiple), size)


def kernel(
    hid, gain_h, qw, qgain_h, ow, kv, pos_h, gdown, gup, dpar_h, dfir_h, dsec_h, upar_h, ufir_h, usec_h,
    new_down, new_up, decoded,
    hidden_all, heads_all, w_raw, o_all, down_t, gd_buf, gu_buf, up_both, kv_buf, kv_f, kv_t, trig, query, low,
    square, result, gain_col, pad_a, out_buf,
    gain, qgain, pos, dpar, dfir, dsec, upar, ufir, usec,
    local_sem, hx_s, hx_r, w_s, w_r, cw_s, cw_r, cc_s, cc_r,
    da_s, da_r, dx_s, dx_r, db_s, db_r, dc_s, dc_r, g_s, g_r, out_s, out_r,
):
    g = lax.axis_index("group")
    t = lax.axis_index("tensor")
    z = lax.div(t, 2)
    xh = lax.rem(t, 2)
    xo = 1 - xh
    core = lax.rem(g, 2)
    sibling = g + 1 - 2 * core
    partner = 2 * z + xo
    right = lax.rem(z + 1, NZ) * 2 + xh
    left = lax.rem(z + NZ - 1, NZ) * 2 + xh
    kvh = lax.div(t, 8)
    beside = {"group": lax.rem(g + NG // 2, NG), "tensor": partner}

    def zm(k):
        return lax.rem(z + 2 * NZ - k, NZ)

    def zp(k):
        return lax.rem(z + k, NZ)

    def remote(src, dst, s_sem, r_sem, device):
        return pltpu.make_async_remote_copy(
            src_ref=src, dst_ref=dst, send_sem=s_sem, recv_sem=r_sem, device_id=device, device_id_type=MESH)

    def lanes(s):
        return pl.ds(s * ROWS, ROWS)

    def lanes_half(h):
        return pl.ds(h * 2 * ROWS, 2 * ROWS)

    barrier = pltpu.get_barrier_semaphore()
    pl.semaphore_signal(barrier, inc=1, device_id={"tensor": partner}, device_id_type=MESH)
    pl.semaphore_signal(barrier, inc=1, device_id=beside, device_id_type=MESH)

    @pl.loop(1, NG)
    def _(k):
        pl.semaphore_signal(barrier, inc=1, device_id={"tensor": 2 * zp(k) + xh}, device_id_type=MESH)
        pl.semaphore_signal(barrier, inc=1, device_id={"group": lax.rem(g + k, NG)}, device_id_type=MESH)

    def own_hidden(s):
        return pltpu.make_async_copy(
            hid.at[s, :, aligned(xh * ROWS, ROWS, 128)],
            hidden_all.at[aligned((2 * z + xh) * FEAT, FEAT, 32), lanes(s)], local_sem.at[s])

    small = [pltpu.make_async_copy(a, b, local_sem.at[4 + i]) for i, (a, b) in enumerate((
        (gain_h, gain), (qgain_h, qgain), (pos_h, pos), (dpar_h, dpar), (dfir_h, dfir), (dsec_h, dsec),
        (upar_h, upar), (ufir_h, ufir), (usec_h, usec)))]
    own_grads = (pltpu.make_async_copy(gdown.at[0], gd_buf.at[0], local_sem.at[13]),
                 pltpu.make_async_copy(gup.at[0], gu_buf.at[0], local_sem.at[14]))
    own_kv = pltpu.make_async_copy(
        kv.at[:, aligned(xh * ROWS, ROWS, 128), :, aligned(kvh * HEAD, HEAD, 128)], kv_buf, local_sem.at[15])
    own_q = pltpu.make_async_copy(qw, w_raw.at[xh], local_sem.at[16])
    own_o = pltpu.make_async_copy(ow, o_all.at[aligned(xh * FEAT, FEAT, 32)], local_sem.at[17])
    for s in range(STEPS):
        own_hidden(s).start()
    for copy in small:
        copy.start()
    for copy in own_grads:
        copy.start()
    own_kv.start()
    own_q.start()
    own_o.start()
    for s in range(STEPS):
        own_hidden(s).wait()

    pl.semaphore_wait(barrier, 2 + 2 * (NG - 1))

    def hx(s, sent):
        return remote(
            hid.at[s, :, aligned(xo * ROWS, ROWS, 128)],
            hidden_all.at[aligned((2 * z + (xh if sent else xo)) * FEAT, FEAT, 32), lanes(s)],
            hx_s.at[s], hx_r.at[s], {"tensor": partner})

    def chunk(phase, zi, j):
        if phase == 0:
            x = xh if j < 2 else xo
            return hidden_all.at[aligned((2 * zi + x) * FEAT, FEAT, 32), lanes_half(j % 2)]
        return heads_all.at[aligned(zi * 2 * HEAD, 2 * HEAD, 256), lanes(j)]

    def ring(phase, k, j, forward, sent):
        back = 1 if sent else 0
        at = phase, k - 1, j
        if forward:
            source, s_sem, r_sem, peer = zm(k - back), cw_s.at[at], cw_r.at[at], right
        else:
            source, s_sem, r_sem, peer = zp(k - back), cc_s.at[at], cc_r.at[at], left
        block = chunk(phase, source, j)
        return remote(block, block, s_sem, r_sem, {"tensor": peer})

    def has(k, j, forward):
        return k < 8 or (j % 2 == 0) == forward

    def ring_start(phase, *which):
        for j in which:
            ring(phase, 1, j, True, True).start()
            ring(phase, 1, j, False, True).start()

    def ring_step(phase, k, j):
        for forward in (True, False):
            if has(k, j, forward):
                ring(phase, k, j, forward, False).wait_recv()
                if k < 8 and has(k + 1, j, forward):
                    ring(phase, k + 1, j, forward, True).start()

    def ring_run(phase, work):
        steps = [(k, j) for k in range(1, 9) for j in range(4)]
        if phase == 0:
            steps = [(1, 0), (1, 1)]
            for k in range(1, 8):
                steps += [(k + 1, 0), (k + 1, 1), (k, 2), (k, 3)]
            steps += [(8, 2), (8, 3)]
        for slot, (k, j) in enumerate(steps):
            ring_step(phase, k, j)
            if phase == 0:
                if slot == 1:
                    start_other()
                for i in range(PIECES):
                    if i * 12 // PIECES == slot:
                        q_piece(i)
                    if i + 12 == slot:
                        o_piece(i)
            for unit in work.get((slot // 4 + 1, slot % 4), ()):
                unit()

    def ring_end(phase):
        for k in range(1, 9):
            for j in range(4):
                for forward in (True, False):
                    if has(k, j, forward):
                        ring(phase, k, j, forward, True).wait_send()

    def grad_copies(k):
        peer = {"group": lax.rem(g + k, NG)}
        return (remote(gdown.at[0], gd_buf.at[k], g_s.at[0, k], g_r.at[0], peer),
                remote(gup.at[0], gu_buf.at[k], g_s.at[1, k], g_r.at[1], peer))

    for s in range(STEPS):
        hx(s, True).start()
    ring_start(0, 0, 1)

    def send_grads(first, last):
        def run():
            @pl.loop(first, last)
            def _(k):
                for copy in grad_copies(k):
                    copy.start()

        return run

    send_grads(1, 5)()

    def q_half(x, c):
        return w_raw.at[x, aligned(c * (WIDTH // 2), WIDTH // 2, 32)]

    def o_half(x, c):
        return o_all.at[aligned(x * FEAT, FEAT, 32), aligned(c * (HQ // 2), HQ // 2, 128)]

    def send_q(sent):
        return remote(qw.at[aligned(core * (WIDTH // 2), WIDTH // 2, 32)], q_half(xh if sent else xo, core),
                      w_s.at[0], w_r.at[0], beside)

    def q_piece(i):
        rows = aligned(core * (WIDTH // 2) + i * FEAT, FEAT, 32)
        remote(qw.at[rows], w_raw.at[xh, rows], w_s.at[0], w_r.at[0], beside).start()

    def o_piece(i):
        part = aligned(core * (HQ // 2) + i * 128, 128, 128)
        remote(ow.at[:, part], o_all.at[aligned(xh * FEAT, FEAT, 32), part], w_s.at[2], w_r.at[2], beside).start()

    def share_q(sent):
        return remote(q_half(xo, core), q_half(xo, core if sent else 1 - core),
                      w_s.at[1], w_r.at[1], {"group": sibling})

    def send_o(sent):
        return remote(ow.at[:, aligned(core * (HQ // 2), HQ // 2, 128)], o_half(xh if sent else xo, core),
                      w_s.at[2], w_r.at[2], beside)

    def share_o(sent):
        return remote(o_half(xo, core), o_half(xo, core if sent else 1 - core),
                      w_s.at[3], w_r.at[3], {"group": sibling})

    def send_u(sent):
        block = up_both.at[:, aligned((xh if sent else xo) * HEAD, HEAD, 128)]
        return remote(block, block, w_s.at[4], w_r.at[4], {"tensor": partner})


    def down_rows(zi, x):
        return down_t.at[aligned((2 * zi + x) * FEAT, FEAT, 32)]

    def down_pair(zi):
        return down_t.at[aligned(zi * 2 * FEAT, 2 * FEAT, 64)]

    def down_along(k):
        return remote(down_rows(g, xh), down_rows(g, xh), da_s.at[k], da_r.at[0], {"tensor": 2 * zp(k) + xh})

    def down_cross(sent):
        block = down_rows(g, xh if sent else xo)
        return remote(block, block, dx_s.at[0], dx_r.at[0], {"tensor": partner})

    def down_share(k, sent):
        block = down_pair(g if sent else lax.rem(g + NG - 2 * k, NG))
        return remote(block, block, db_s.at[k], db_r.at[k], {"group": lax.rem(g + 2 * k, NG)})

    def down_pass(k, sent):
        block = down_pair(lax.rem((g if sent else sibling) + NG - 2 * k, NG))
        return remote(block, block, dc_s.at[k], dc_r.at[k], {"group": sibling})

    def down_first_part():
        @pl.when(z != g)
        def _():
            down_along(1).wait_recv()

        down_cross(True).start()

    def down_second_part():
        down_cross(False).wait_recv()

        down_share(1, True).start()

    def down_third_part():
        @pl.loop(1, NG // 2)
        def _(k):
            down_share(k, False).wait_recv()
            down_pass(k, True).start()

    def down_wait():
        @pl.loop(0, NG // 2)
        def _(k):
            down_pass(k, False).wait_recv()

    def do_gain(i):
        for c in range(8 * i, 8 * i + 8):
            gain_col[c * 128 : (c + 1) * 128, :] = jnp.broadcast_to(gain[c : c + 1, :], (128, 128)).T

    def do_trig(s):
        index = lax.broadcasted_iota(jnp.int32, (HEAD // 2, ROWS), 0)
        fine, coarse = lax.rem(index, 8), lax.div(index, 8)
        fine_part = jnp.ones((HEAD // 2, ROWS), F32)
        coarse_part = fine_part
        for i in range(1, 8):
            fine_part = jnp.where(fine == i, float(rope_base ** (-2.0 * i / HEAD)), fine_part)
            coarse_part = jnp.where(coarse == i, float(rope_base ** (-16.0 * i / HEAD)), coarse_part)
        angle = pos[s : s + 1, aligned(xh * ROWS, ROWS, 128)].astype(F32) * (fine_part * coarse_part)
        trig[0, :, lanes(s)] = jnp.cos(angle)
        trig[1, :, lanes(s)] = jnp.sin(angle)

    def do_kv(i, j):
        if j == 0:
            kv_f[...] = kv_buf[i].astype(F32)
        for c in range(4 * j, 4 * j + 4):
            kv_t[i, c] = kv_f[:, c, :].T

    def do_w(x, i):
        part = pl.ds(i * 1024, 1024)
        w_raw[x, part, :] = (w_raw[x, part, :].astype(F32) * gain_col[part, :]).astype(BF16)

    def do_sums():
        every = pl.ds(1, NG - 1)
        for copy in own_grads:
            copy.wait()
        pltpu.make_async_copy(gd_buf.at[every], gd_buf.at[every], g_r.at[0]).wait()
        pltpu.make_async_copy(gu_buf.at[every], gu_buf.at[every], g_r.at[1]).wait()
        down_sum = gd_buf[0].astype(F32)
        up_sum = gu_buf[0].astype(F32)
        for k in range(1, NG):
            down_sum += gd_buf[k].astype(F32)
            up_sum += gu_buf[k].astype(F32)
        down = adamw(dpar[...], dfir[...], dsec[...], down_sum)
        up = adamw(upar[...], ufir[...], usec[...], up_sum)
        new_down[...] = down
        new_up[...] = up
        up_both[:, aligned(xh * HEAD, HEAD, 128)] = up

        @pl.when(z == g)
        def _():
            pad_a[...] = jnp.zeros_like(pad_a)
            pad_a[:RANK, :FEAT] = down
            pad_a[RANK:, :FEAT] = down
            scaled = pad_a[...].T[:FEAT, :] * gain_col[aligned(t * FEAT, FEAT, 32), :]
            hi = scaled.astype(BF16).astype(F32)
            lane = lax.broadcasted_iota(jnp.int32, (FEAT, 2 * RANK), 1)
            down_t[aligned((2 * g + xh) * FEAT, FEAT, 32), :] = jnp.where(lane < RANK, hi, scaled - hi).astype(BF16)

            @pl.loop(1, NZ)
            def _(k):
                down_along(k).start()

        send_u(True).start()

    across = (((0,), (0,)), ((), ()))

    everything = pl.ds(0, TOK)

    def q_block(zi, part=everything):
        rows = aligned(zi * 2 * FEAT, 2 * FEAT, 64)
        block = hidden_all[rows, part]
        for x in range(2):
            query[x * HEAD : (x + 1) * HEAD, part] += lax.dot_general(
                w_raw[x, rows, :], block, across, preferred_element_type=F32)
        wide = block.astype(F32)
        square[:, part] += jnp.sum((wide * wide).reshape(2 * FEAT // 8, 8, part.size), axis=0)

    def low_block(zi, part=everything):
        rows = aligned(zi * 2 * FEAT, 2 * FEAT, 64)
        low[:, part] += lax.dot_general(
            down_t[rows, :], hidden_all[rows, part], across, preferred_element_type=F32)

    def clear():
        query[...] = jnp.zeros_like(query)
        low[...] = jnp.zeros_like(low)
        square[...] = jnp.zeros_like(square)

    def finish_query(h):
        part = lanes_half(h)
        inverse = lax.rsqrt(jnp.sum(square[:, part], axis=0, keepdims=True) * (1.0 / WIDTH) + norm_eps)
        delta = lax.dot_general(
            up_both[...], low[:RANK, part] + low[RANK:, part], across,
            precision=lax.Precision.HIGHEST, preferred_element_type=F32)
        query[:, part] = (query[:, part] + delta * float(1.0 / np.sqrt(RANK * WIDTH))) * inverse

    half = HEAD // 2

    def attend(s):
        qgain_col = jnp.broadcast_to(qgain[...], (HEAD, HEAD)).T
        for x in range(2):
            q = query[x * HEAD : (x + 1) * HEAD, lanes(s)]
            q = q * lax.rsqrt(jnp.sum(q * q, axis=0, keepdims=True) * (1.0 / HEAD) + norm_eps) * qgain_col
            cosine, sine = trig[0, :, lanes(s)], trig[1, :, lanes(s)]
            first, second = q[:half], q[half:]
            rotated = jnp.concatenate(
                [first * cosine - second * sine, second * cosine + first * sine], axis=0)
            rotated = rotated.astype(BF16).astype(F32)
            scores = jnp.concatenate(
                [jnp.sum(rotated * kv_t[0, c], axis=0, keepdims=True) for c in range(CACHE)], axis=0)
            scores = scores * float(1.0 / np.sqrt(HEAD))
            expo = jnp.exp(scores - jnp.max(scores, axis=0, keepdims=True))
            weights = (expo / jnp.sum(expo, axis=0, keepdims=True)).astype(BF16).astype(F32)
            total = weights[0:1] * kv_t[1, 0]
            for c in range(1, CACHE):
                total += weights[c : c + 1] * kv_t[1, c]
            heads_all[aligned((2 * z + x) * HEAD, HEAD, 128), lanes(s)] = total.astype(BF16)

    def o_start():
        result[...] = hidden_all[aligned(z * 2 * FEAT, 2 * FEAT, 64), :].astype(F32)

    def o_block(zi, part=everything):
        rows = aligned(zi * 2 * HEAD, 2 * HEAD, 256)
        result[:, part] += jnp.dot(o_all[:, rows], heads_all[rows, part], preferred_element_type=F32)

    def out_copy(s, x):
        return remote(
            out_buf.at[s], decoded.at[s, :, aligned(x * ROWS, ROWS, 128)],
            out_s.at[s], out_r.at[s], {"tensor": partner})

    def finish(s):
        o_block(zm(8), lanes(s))
        out_buf[s] = result[aligned(xo * FEAT, FEAT, 32), lanes(s)].astype(BF16)
        out_copy(s, xh).start()
        decoded[s, :, aligned(xh * ROWS, ROWS, 128)] = result[aligned(xh * FEAT, FEAT, 32), lanes(s)].astype(BF16)

    order = [lambda: z] + [lambda f=f, k=k: f(k) for k in range(1, 8) for f in (zm, zp)]

    def blocks(kind, first, last):
        def run():
            for i in range(first, last):
                kind(order[i]())

        return run

    def wait_small():
        for copy in small:
            copy.wait()

    def q_arrived():
        send_q(False).wait_recv()
        share_q(True).start()

    def q_shared():
        share_q(False).wait_recv()
        share_q(True).wait_send()

    def o_arrived():
        send_o(False).wait_recv()
        share_o(True).start()

    def o_shared():
        own_o.wait()
        share_o(False).wait_recv()

    def start_other():
        for h in range(2):
            hx(2 * h, False).wait_recv()
            hx(2 * h + 1, False).wait_recv()
            ring_start(0, 2 + h)

    def last_hidden(h):
        q_block(zm(8), lanes_half(h))
        low_block(zm(8), lanes_half(h))
        finish_query(h)
        for s in (2 * h, 2 * h + 1):
            attend(s)
            ring_start(1, s)

    ring_run(0, {
        (1, 0): [send_grads(5, 9), wait_small, lambda: do_gain(0)],
        (1, 1): [send_grads(9, 13)],
        (1, 2): [send_grads(13, 16), lambda: do_gain(1), lambda: do_gain(2)],
        (1, 3): [lambda: do_gain(3), lambda: do_gain(4)],
        (2, 0): [lambda: do_trig(0)],
        (2, 1): [lambda: do_trig(1)],
        (2, 2): [lambda: do_trig(2)],
        (2, 3): [lambda: do_trig(3)],
        (3, 0): [do_sums],
        (3, 1): [own_kv.wait, lambda: do_kv(0, 0)],
        (3, 2): [lambda: do_kv(0, 1)],
        (3, 3): [lambda: do_kv(1, 0)],
        (4, 0): [down_first_part],
        (4, 1): [lambda: do_kv(1, 1)],
        (4, 2): [own_q.wait, lambda: do_w(xh, 0), lambda: do_w(xh, 1)],
        (4, 3): [lambda: do_w(xh, 2), lambda: do_w(xh, 3)],
        (5, 0): [down_second_part, q_arrived],
        (5, 1): [lambda: down_share(2, True).start(), lambda: down_share(3, True).start(), lambda: do_w(xh, 4), clear],
        (5, 2): [lambda: down_share(4, True).start(), lambda: down_share(5, True).start(),
                 q_shared, lambda: do_w(xo, 0)],
        (5, 3): [lambda: down_share(6, True).start(), lambda: down_share(7, True).start(),
                 lambda: do_w(xo, 1), lambda: do_w(xo, 2)],
        (6, 0): [lambda: down_pass(0, True).start(), lambda: do_w(xo, 3), lambda: do_w(xo, 4)],
        (6, 1): [blocks(q_block, 0, 2)],
        (6, 2): [blocks(q_block, 2, 4)],
        (6, 3): [down_third_part, blocks(q_block, 4, 5)],
        (7, 0): [blocks(q_block, 5, 7)],
        (7, 1): [blocks(q_block, 7, 9)],
        (7, 2): [down_wait, blocks(q_block, 9, 11), blocks(low_block, 0, 1)],
        (7, 3): [blocks(low_block, 1, 6)],
        (8, 0): [blocks(low_block, 6, 11)],
        (8, 1): [blocks(q_block, 11, 13), blocks(low_block, 11, 13), lambda: send_u(False).wait_recv(),
                 blocks(q_block, 13, 15), blocks(low_block, 13, 15)],
        (8, 2): [lambda: last_hidden(0)],
        (8, 3): [lambda: last_hidden(1)],
    })
    ring_run(1, {
        (1, 0): [o_arrived],
        (1, 1): [o_start],
        (1, 3): [o_shared],
        (2, 0): [blocks(o_block, 0, 1)],
        (2, 2): [blocks(o_block, 1, 3)],
        (3, 0): [blocks(o_block, 3, 4)],
        (3, 2): [blocks(o_block, 4, 5)],
        (4, 0): [blocks(o_block, 5, 6)],
        (4, 2): [blocks(o_block, 6, 7)],
        (5, 0): [blocks(o_block, 7, 8)],
        (5, 2): [blocks(o_block, 8, 9)],
        (6, 0): [blocks(o_block, 9, 10)],
        (6, 2): [blocks(o_block, 10, 11)],
        (7, 0): [blocks(o_block, 11, 12)],
        (7, 2): [blocks(o_block, 12, 13)],
        (7, 3): [blocks(o_block, 13, 15)],
        (8, 0): [lambda: finish(0)],
        (8, 1): [lambda: finish(1)],
        (8, 2): [lambda: finish(2)],
        (8, 3): [lambda: finish(3)],
    })

    for phase in range(2):
        ring_end(phase)
    for s in range(STEPS):
        hx(s, True).wait_send()
    for copy in (send_q, send_o, share_o, send_u, down_cross):
        copy(True).wait_send()

    @pl.when(z == g)
    def _():
        @pl.loop(1, NZ)
        def _(k):
            down_along(k).wait_send()

    @pl.loop(1, NG)
    def _(k):
        for copy in grad_copies(k):
            copy.wait_send()

    down_pass(0, True).wait_send()

    @pl.loop(1, NG // 2)
    def _(k):
        down_share(k, True).wait_send()
        down_pass(k, True).wait_send()

    for s in range(STEPS):
        out_copy(s, xh).wait_send()
        out_copy(s, xo).wait_recv()


def hand_over(*refs):
    count = len(refs) // 2
    for source, target in zip(refs[:count], refs[count:]):
        target[...] = source[...]


def body(
    hidden_in, norm_gain, q_weight, q_gain, o_weight, kv_cache, positions, grad_down, grad_up,
    down_param, down_first, down_second, up_param, up_first, up_second,
):
    vmem = pl.BlockSpec(memory_space=pltpu.VMEM)
    anywhere = pl.BlockSpec(memory_space=pl.ANY)
    dma = pltpu.SemaphoreType.DMA
    shapes = (
        jax.ShapeDtypeStruct((RANK, FEAT), F32),
        jax.ShapeDtypeStruct((RANK, HEAD), F32),
        jax.ShapeDtypeStruct((STEPS, FEAT, 2 * ROWS), BF16),
    )
    results = pl.pallas_call(
        kernel,
        out_shape=shapes,
        in_specs=[anywhere] * 15,
        out_specs=(vmem, vmem, vmem),
        scratch_shapes=[
            pltpu.VMEM((WIDTH, TOK), BF16),
            pltpu.VMEM((HQ, TOK), BF16),
            pltpu.VMEM((2, WIDTH, HEAD), BF16),
            pltpu.VMEM((2 * FEAT, HQ), BF16),
            pltpu.VMEM((WIDTH, 2 * RANK), BF16),
            pltpu.VMEM((NG, RANK, FEAT), BF16),
            pltpu.VMEM((NG, RANK, HEAD), BF16),
            pltpu.VMEM((RANK, 2 * HEAD), F32),
            pltpu.VMEM((2, ROWS, CACHE, HEAD), BF16),
            pltpu.VMEM((ROWS, CACHE, HEAD), F32),
            pltpu.VMEM((2, CACHE, HEAD, ROWS), F32),
            pltpu.VMEM((2, HEAD // 2, TOK), F32),
            pltpu.VMEM((2 * HEAD, TOK), F32),
            pltpu.VMEM((2 * RANK, TOK), F32),
            pltpu.VMEM((8, TOK), F32),
            pltpu.VMEM((2 * FEAT, TOK), F32),
            pltpu.VMEM((WIDTH, 128), F32),
            pltpu.VMEM((2 * RANK, 256), F32),
            pltpu.VMEM((STEPS, FEAT, ROWS), BF16),
            pltpu.VMEM((WIDTH // 128, 128), F32),
            pltpu.VMEM((1, HEAD), F32),
            pltpu.VMEM((STEPS, 2 * ROWS), jnp.int32),
            pltpu.VMEM((RANK, FEAT), F32), pltpu.VMEM((RANK, FEAT), F32), pltpu.VMEM((RANK, FEAT), F32),
            pltpu.VMEM((RANK, HEAD), F32), pltpu.VMEM((RANK, HEAD), F32), pltpu.VMEM((RANK, HEAD), F32),
            dma((18,)),
            dma((STEPS,)), dma((STEPS,)),
            dma((5,)), dma((5,)),
            dma((2, 8, 4)), dma((2, 8, 4)), dma((2, 8, 4)), dma((2, 8, 4)),
            dma((NZ,)), dma((1,)), dma((1,)), dma((1,)),
            dma((NG // 2,)), dma((NG // 2,)), dma((NG // 2,)), dma((NG // 2,)),
            dma((2, NG)), dma((2,)),
            dma((STEPS,)), dma((STEPS,)),
        ],
        compiler_params=pltpu.CompilerParams(
            collective_id=0, has_side_effects=True, vmem_limit_bytes=56 * 1024 * 1024),
        cost_estimate=pl.CostEstimate(flops=3_000_000_000, bytes_accessed=10_000_000, transcendentals=100_000),
    )(
        jnp.transpose(hidden_in, (0, 2, 1)), norm_gain.reshape(WIDTH // 128, 128), q_weight,
        q_gain.reshape(1, HEAD), jnp.transpose(o_weight), kv_cache, positions, grad_down, grad_up,
        down_param, down_first, down_second, up_param, up_first, up_second,
    )
    new_down, new_up, decoded = pl.pallas_call(
        hand_over,
        out_shape=shapes,
        in_specs=[vmem] * 3,
        out_specs=(vmem,) * 3,
    )(*results)
    return new_down, new_up, jnp.transpose(decoded, (0, 2, 1))


def solution(mesh):
    in_specs = (
        P(None, "group", "tensor"),
        P(),
        P(None, "tensor"),
        P(),
        P(None, "tensor"),
        P(None, "group", None, None),
        P(None, "group"),
        P("group", None, "tensor"),
        P("group", None, "tensor"),
        P(None, "tensor"),
        P(None, "tensor"),
        P(None, "tensor"),
        P(None, "tensor"),
        P(None, "tensor"),
        P(None, "tensor"),
    )
    out_specs = (P(None, "tensor"), P(None, "tensor"), P(None, "group", "tensor"))
    return jax.shard_map(body, mesh=mesh, in_specs=in_specs, out_specs=out_specs, check_vma=False)
```

time: 141 us -> 134 us (0.950); the launches traced: 141 us -> 131 us
  local copies, waits for them, and re-layouts: 5.91 us -> 0 us
  Pallas kernels: 134 us -> 131 us
    unnamed x3 -> x0, local copies, waits for them, and re-layouts: 4.56 us -> none
    pallas_call x1 -> x2, Pallas kernels: 134 us -> 131 us  [the longest x1 129 us: body(): pl.pallas_call(kernel, out_shape=shapes, in_specs=[anywhere] * 15, out_sp...]
where the time goes in v3:
time: 134 us; the launch traced here: 131 us
  Pallas kernels  131 us (98%)
    pallas_call x1, Pallas kernels, body(): pl.pallas_call(kernel, out_shape=shapes, in_specs=[anywhere] * 15, out_sp...  129 us

profile of v3, /device:TPU:1, one launch (start us, length us, event | category | flops | bytes accessed | tf_op | source)
XLA Modules:
  0.0 131.4 jit_solution(3267839292544024362)
XLA Ops:
  0.6 128.9 %shard_map.166 = (f32[64,160]{1,0:T(8,128)}, f32[64,128]{1,0:T(8,128)}, bf16[4,160,256]{2,1,0:T(8,128)(2,1)}) custom-call(bf16[4,160,256]{2,1,0:T(8,128)(2,1)} %bitcast.6, f32[40,128]{1,0:T(8,128)} %bitcast.8, bf16[5120,128]{1,0:T(8,128)(2,1)} %qw.1, f32[1,128]{1,0:T(1,128)} %bitcast.9, bf16[160,4096]{1,0:T(8,128)(2,1)} %bitcast.5, ...), custom_call_target="tpu_custom_call" | custom-call | flops 3000000000 | bytes 10000000 | tf_op jit(solution)/shard_map/pallas_call | solution.py:567
  129.6 1.8 %shard_map.167 = (f32[64,160]{1,0:T(8,128)}, f32[64,128]{1,0:T(8,128)}, bf16[4,160,256]{2,1,0:T(8,128)(2,1)}) custom-call(f32[64,160]{1,0:T(8,128)} %get-tuple-element.9.refs_0_, f32[64,128]{1,0:T(8,128)} %get-tuple-element.10.refs_1_, bf16[4,160,256]{2,1,0:T(8,128)(2,1)} %get-tuple-element.11.refs_2_), custom_call_target="tpu_custom_call" | custom-call | tf_op jit(solution)/shard_map/pallas_call | solution.py:614

commit v4 on v3

--- a/solution.py
+++ b/solution.py
@@ -465,28 +465,28 @@
         (2, 1): [lambda: do_trig(1)],
         (2, 2): [lambda: do_trig(2)],
         (2, 3): [lambda: do_trig(3)],
-        (3, 0): [do_sums],
-        (3, 1): [own_kv.wait, lambda: do_kv(0, 0)],
+        (3, 0): [own_kv.wait, lambda: do_kv(0, 0)],
+        (3, 1): [do_sums],
         (3, 2): [lambda: do_kv(0, 1)],
         (3, 3): [lambda: do_kv(1, 0)],
-        (4, 0): [down_first_part],
+        (4, 0): [],
         (4, 1): [lambda: do_kv(1, 1)],
-        (4, 2): [own_q.wait, lambda: do_w(xh, 0), lambda: do_w(xh, 1)],
+        (4, 2): [down_first_part, own_q.wait, lambda: do_w(xh, 0), lambda: do_w(xh, 1)],
         (4, 3): [lambda: do_w(xh, 2), lambda: do_w(xh, 3)],
-        (5, 0): [down_second_part, q_arrived],
-        (5, 1): [lambda: down_share(2, True).start(), lambda: down_share(3, True).start(), lambda: do_w(xh, 4), clear],
-        (5, 2): [lambda: down_share(4, True).start(), lambda: down_share(5, True).start(),
+        (5, 0): [q_arrived],
+        (5, 1): [down_second_part, lambda: down_share(2, True).start(), lambda: do_w(xh, 4), clear],
+        (5, 2): [lambda: down_share(3, True).start(), lambda: down_share(4, True).start(), lambda: down_share(5, True).start(),
                  q_shared, lambda: do_w(xo, 0)],
         (5, 3): [lambda: down_share(6, True).start(), lambda: down_share(7, True).start(),
                  lambda: do_w(xo, 1), lambda: do_w(xo, 2)],
         (6, 0): [lambda: down_pass(0, True).start(), lambda: do_w(xo, 3), lambda: do_w(xo, 4)],
         (6, 1): [blocks(q_block, 0, 2)],
         (6, 2): [blocks(q_block, 2, 4)],
-        (6, 3): [down_third_part, blocks(q_block, 4, 5)],
-        (7, 0): [blocks(q_block, 5, 7)],
+        (6, 3): [blocks(q_block, 4, 5)],
+        (7, 0): [down_third_part, blocks(q_block, 5, 7)],
         (7, 1): [blocks(q_block, 7, 9)],
-        (7, 2): [down_wait, blocks(q_block, 9, 11), blocks(low_block, 0, 1)],
-        (7, 3): [blocks(low_block, 1, 6)],
+        (7, 2): [blocks(q_block, 9, 11)],
+        (7, 3): [down_wait, blocks(low_block, 0, 6)],
         (8, 0): [blocks(low_block, 6, 11)],
         (8, 1): [blocks(q_block, 11, 13), blocks(low_block, 11, 13), lambda: send_u(False).wait_recv(),
                  blocks(q_block, 13, 15), blocks(low_block, 13, 15)],

time: 134 us -> 134 us (level)
  the two profiles are of different devices: /device:TPU:1 before, /device:TPU:8 now
where the time goes in v4:
time: 134 us
  Pallas kernels  133 us (99%)
    pallas_call x1, Pallas kernels, body(): pl.pallas_call(kernel, out_shape=shapes, in_specs=[anywhere] * 15, out_sp...  131 us

profile of v4, /device:TPU:8, one launch (start us, length us, event | category | flops | bytes accessed | tf_op | source)
XLA Modules:
  0.0 133.7 jit_solution(6353303756359513336)
XLA Ops:
  0.6 131.2 %shard_map.166 = (f32[64,160]{1,0:T(8,128)}, f32[64,128]{1,0:T(8,128)}, bf16[4,160,256]{2,1,0:T(8,128)(2,1)}) custom-call(bf16[4,160,256]{2,1,0:T(8,128)(2,1)} %bitcast.6, f32[40,128]{1,0:T(8,128)} %bitcast.8, bf16[5120,128]{1,0:T(8,128)(2,1)} %qw.1, f32[1,128]{1,0:T(1,128)} %bitcast.9, bf16[160,4096]{1,0:T(8,128)(2,1)} %bitcast.5, ...), custom_call_target="tpu_custom_call" | custom-call | flops 3000000000 | bytes 10000000 | tf_op jit(solution)/shard_map/pallas_call | solution.py:567
  131.9 1.8 %shard_map.167 = (f32[64,160]{1,0:T(8,128)}, f32[64,128]{1,0:T(8,128)}, bf16[4,160,256]{2,1,0:T(8,128)(2,1)}) custom-call(f32[64,160]{1,0:T(8,128)} %get-tuple-element.9.refs_0_, f32[64,128]{1,0:T(8,128)} %get-tuple-element.10.refs_1_, bf16[4,160,256]{2,1,0:T(8,128)(2,1)} %get-tuple-element.11.refs_2_), custom_call_target="tpu_custom_call" | custom-call | tf_op jit(solution)/shard_map/pallas_call | solution.py:614
